TPU v7x, 512 devices: a whole 4x4x16 slice. The times are simulated.
512 devices in a mesh: leaf: 32 (over x, y, core), front: 16 (over z).
Axes of the slice: x: 4, y: 4, z: 16, core: 2. Of those that a mesh axis runs over, the one named last changes fastest.
Arguments:
- panel_0: float32 [2, 1024, 1024], P(None, 'front', 'leaf'), as said below
- panel_1: float32 [2, 1024, 2048], P(None, 'front', 'leaf'), as said below
- panel_2: float32 [2, 1024, 4096], P(None, 'front', 'leaf'), as said below
- panel_3: float32 [2, 1024, 8192], P(None, 'front', 'leaf'), as said below
- load_0: float32 [1024, 128], P('leaf'), may hold values from -6 to 6
- load_1: float32 [2048, 128], P('leaf'), may hold values from -6 to 6
- load_2: float32 [4096, 128], P('leaf'), may hold values from -6 to 6
- load_3: float32 [8192, 128], P('leaf'), may hold values from -6 to 6
- inflow: float32 [8, 1024, 128], P(None, 'front'), may hold values from -6 to 6
- above_solution: float32 [1024, 128], replicated, may hold values from -6 to 6
- block_maps: int32 [14, 16], replicated, may hold values from 0 to 31, as said below
Outputs:
- solution_0: float32 [1024, 128], P(('leaf', 'front'))
- solution_1: float32 [2048, 128], P(('leaf', 'front'))
- solution_2: float32 [4096, 128], P(('leaf', 'front'))
- solution_3: float32 [8192, 128], P(('leaf', 'front'))
- top_update: float32 [1024, 128], P('front')
Inputs may be any that keep to these rules, and one draw needn't show every extreme that they name: `block_maps`: the 16 entries of each row are distinct. `panel_0`: within each front the pivot block K is lower triangular with diagonal entries of 0.8 to 1.25. `panel_1`: within each front the pivot block K is lower triangular with diagonal entries of 0.8 to 1.25. `panel_2`: within each front the pivot block K is lower triangular with diagonal entries of 0.8 to 1.25. `panel_3`: within each front the pivot block K is lower triangular with diagonal entries of 0.8 to 1.25.
All inputs are finite; a program needn't handle non-finite values.
Results may differ from a plain program's by a relative error of at most 0.00013.
Values sent between devices are 32-bit elements; how exact they have to be, the bound alone decides.
No kernel may reach another device: no remote copies, remote signals or barrier semaphores. Data moves between devices by JAX's collectives and lax.ppermute only.
A program may use at most 64 MiB of HBM per device.

v0:
```python
import jax
import jax.numpy as jnp
from jax import lax
from jax.sharding import PartitionSpec as P

exact_precision = lax.Precision.HIGHEST


def partner_2(value, axis, distance):
    mask = 2**distance
    pairs = [(source, source ^ mask) for source in range(lax.axis_size(axis))]
    return lax.ppermute(value, axis, pairs)


def group_total(partial_sum, group_bits, level_id):
    leaf_pos = lax.axis_index("leaf")
    group_count = 1 << level_id
    slot_id = leaf_pos >> group_bits
    chosen = (jnp.arange(group_count, dtype=jnp.int32) == slot_id).astype(jnp.float32)
    spread_out = chosen.reshape((group_count,) + (1,) * partial_sum.ndim) * partial_sum[None]
    totals = lax.psum(spread_out, "leaf")
    return lax.dynamic_index_in_dim(totals, slot_id, 0, keepdims=False)


def group_concat(column_block, group_bits):
    leaf_pos = lax.axis_index("leaf")
    for section_bit in range(group_bits):
        partner = partner_2(column_block, "leaf", section_bit)
        upper_half = leaf_pos >> section_bit & 1 == 1
        column_block = jnp.where(
            upper_half,
            jnp.concatenate([partner, column_block], 0),
            jnp.concatenate([column_block, partner], 0),
        )
    return column_block


def place_blocks(map_row, values, block_rows):
    block_count = map_row.shape[0]
    targets = jnp.arange(2 * block_count, dtype=jnp.int32)
    selector_matrix = (targets[:, None] == map_row[None, :]).astype(jnp.float32)
    factor_blocks = values.reshape(block_count, block_rows, values.shape[1])
    return jnp.einsum("du,uye->dye", selector_matrix, factor_blocks, precision=exact_precision)


def lift_update(update_block, level_id, group_bits, block_maps, sep_rows):
    leaf_pos = lax.axis_index("leaf")
    front_pos = lax.axis_index("front")
    block_rows = update_block.shape[0]
    block_count = sep_rows // block_rows
    group_size = 1 << group_bits
    child_id = leaf_pos >> group_bits
    base_row = (1 << level_id) - 2
    own_map = lax.dynamic_index_in_dim(block_maps, base_row + child_id, 0, keepdims=False)
    parent_pos = leaf_pos % (2 * group_size)
    parent_rows = sep_rows // (2 * group_size)
    other_map = lax.dynamic_index_in_dim(block_maps, base_row + (child_id ^ 1), 0, keepdims=False)
    partner_block = partner_2(update_block, "leaf", group_bits)
    own_full, other_full = (
        lax.all_gather(update_block, "front", axis=0, tiled=True),
        lax.all_gather(partner_block, "front", axis=0, tiled=True),
    )
    placed = place_blocks(own_map, own_full, block_rows) + place_blocks(
        other_map, other_full, block_rows
    )
    separator = placed[:block_count].reshape(sep_rows, -1)
    sep_part = lax.dynamic_slice_in_dim(separator, parent_pos * parent_rows, parent_rows, 0)
    border = lax.dynamic_index_in_dim(placed, block_count + front_pos, 0, keepdims=False)
    return (sep_part, border)


def on_device(
    panel_0,
    panel_1,
    panel_2,
    panel_3,
    load_0,
    load_1,
    load_2,
    load_3,
    inflow,
    above_solution,
    block_maps,
):
    panels = (panel_0, panel_1, panel_2, panel_3)
    load_list = (load_0, load_1, load_2, load_3)
    level_count = len(panels)
    leaf_pos = lax.axis_index("leaf")
    front_pos = lax.axis_index("front")
    front_count = lax.axis_size("front")
    total_bits = lax.axis_size("leaf").bit_length() - 1
    block_rows = panel_0.shape[1]
    sep_rows = block_rows * front_count
    solved = [None] * level_count
    lifted = None
    top_block = None
    for level_id in range(level_count - 1, -1, -1):
        group_bits = total_bits - level_id
        right_side = load_list[level_id]
        if level_id == level_count - 1:
            front_id = leaf_pos >> group_bits
            border = lax.dynamic_index_in_dim(inflow, front_id, 0, keepdims=False)
        else:
            right_side = right_side + lifted[0]
            border = lifted[1]
        partial_sum = jnp.einsum(
            "ksc,cr->ksr", panels[level_id], right_side, precision=exact_precision
        )
        totals = group_total(partial_sum, group_bits, level_id)
        solved[level_id] = totals[0]
        update_block = border - totals[1]
        if level_id > 0:
            lifted = lift_update(update_block, level_id, group_bits, block_maps, sep_rows)
        else:
            top_block = update_block
    upper_full = above_solution
    upper_block = lax.dynamic_slice_in_dim(above_solution, front_pos * block_rows, block_rows, 0)
    targets = jnp.arange(2 * front_count, dtype=jnp.int32)
    pieces = []
    for level_id in range(level_count):
        group_bits = total_bits - level_id
        stacked = jnp.stack([solved[level_id], -upper_block])
        partial_sum = jnp.einsum(
            "ksc,ksr->cr", panels[level_id], stacked, precision=exact_precision
        )
        column_block = lax.psum(partial_sum, "front")
        span_rows = column_block.shape[0] // front_count
        pieces.append(lax.dynamic_slice_in_dim(column_block, front_pos * span_rows, span_rows, 0))
        if level_id < level_count - 1:
            full_solution = group_concat(column_block, group_bits)
            ancestor_blocks = jnp.concatenate([full_solution, upper_full], 0).reshape(
                2 * front_count, block_rows, -1
            )
            child_id = leaf_pos >> group_bits - 1
            child_map = lax.dynamic_index_in_dim(
                block_maps, (2 << level_id) - 2 + child_id, 0, keepdims=False
            )
            selector_matrix = (child_map[:, None] == targets[None, :]).astype(jnp.float32)
            upper_factor_blocks = jnp.einsum(
                "gq,qzk->gzk", selector_matrix, ancestor_blocks, precision=exact_precision
            )
            upper_full = upper_factor_blocks.reshape(sep_rows, -1)
            upper_block = lax.dynamic_index_in_dim(
                upper_factor_blocks, front_pos, 0, keepdims=False
            )
    return (pieces[0], pieces[1], pieces[2], pieces[3], top_block)


def solution(mesh):
    in_specs = (
        P(None, "front", "leaf"),
        P(None, "front", "leaf"),
        P(None, "front", "leaf"),
        P(None, "front", "leaf"),
        P("leaf", None),
        P("leaf", None),
        P("leaf", None),
        P("leaf", None),
        P(None, "front", None),
        P(),
        P(),
    )
    out_specs = (
        P(("leaf", "front"), None),
        P(("leaf", "front"), None),
        P(("leaf", "front"), None),
        P(("leaf", "front"), None),
        P("front", None),
    )
    return jax.shard_map(
        on_device, mesh=mesh, in_specs=in_specs, out_specs=out_specs, check_vma=False
    )
```

profile of v0, /device:TPU:2, one launch (start us, length us, event | category | flops | bytes accessed | tf_op | source)
XLA Modules:
  0.0 1208.8 jit_solution(1407500976551751530)
XLA Ops:
  8.1 1.2 fusion.16
  11.1 138.3 %all-reduce.7.cloned.1.call-done = f32[8,2,64,128]{3,2,1,0:T(8,128)} async-done(((f32[8,2,64,128]{3,2,1,0:T(8,128)}), f32[8,2,64,128]{3,2,1,0:T(8,128)}) %all-reduce.7.cloned.1.call-update) | async-done | bytes 524304 | tf_op jit(solution)/shard_map/psum | solution.py:21
  150.2 4.2 collective-permute-start
  154.4 33.1 %all_gather.18 = f32[1024,128]{1,0:T(8,128)S(1)} all-gather(f32[64,128]{1,0:T(8,128)S(1)} %fusion.32), channel_id=1, replica_groups=mesh['leaf'=32,'front'=16] {'front'}, dimensions={0}, use_global_device_ids=true | all-gather | bytes 557056 | tf_op jit(solution)/shard_map/all_gather | solution.py:60
  188.5 30.6 %all_gather.19 = f32[1024,128]{1,0:T(8,128)S(1)} all-gather(f32[64,128]{1,0:T(8,128)S(1)} %collective-permute-done), channel_id=1, replica_groups=mesh['leaf'=32,'front'=16] {'front'}, dimensions={0}, use_global_device_ids=true | all-gather | bytes 557056 | tf_op jit(solution)/shard_map/all_gather | solution.py:61
  219.1 1.0 convolution_add_fusion.2
  222.2 127.9 %all-reduce.9.cloned.1.call-done = f32[4,2,64,128]{3,2,1,0:T(8,128)} async-done(((f32[4,2,64,128]{3,2,1,0:T(8,128)}), f32[4,2,64,128]{3,2,1,0:T(8,128)}) %all-reduce.9.cloned.1.call-update) | async-done | bytes 262160 | tf_op jit(solution)/shard_map/psum | solution.py:21
  350.8 3.0 collective-permute-start.1
  353.8 33.6 %all_gather.20 = f32[1024,128]{1,0:T(8,128)S(1)} all-gather(f32[64,128]{1,0:T(8,128)S(1)} %fusion.31), channel_id=1, replica_groups=mesh['leaf'=32,'front'=16] {'front'}, dimensions={0}, use_global_device_ids=true | all-gather | bytes 557056 | tf_op jit(solution)/shard_map/all_gather | solution.py:60
  388.3 30.1 %all_gather.21 = f32[1024,128]{1,0:T(8,128)S(1)} all-gather(f32[64,128]{1,0:T(8,128)S(1)} %collective-permute-done.1), channel_id=1, replica_groups=mesh['leaf'=32,'front'=16] {'front'}, dimensions={0}, use_global_device_ids=true | all-gather | bytes 557056 | tf_op jit(solution)/shard_map/all_gather | solution.py:61
  421.3 126.1 %all-reduce.11.cloned.1.call-done = f32[2,2,64,128]{3,2,1,0:T(8,128)} async-done(((f32[2,2,64,128]{3,2,1,0:T(8,128)}), f32[2,2,64,128]{3,2,1,0:T(8,128)}) %all-reduce.11.cloned.1.call-update) | async-done | bytes 131088 | tf_op jit(solution)/shard_map/psum | solution.py:21
  548.2 5.2 collective-permute-start.2
  553.4 33.3 %all_gather.22 = f32[1024,128]{1,0:T(8,128)S(1)} all-gather(f32[64,128]{1,0:T(8,128)S(1)} %fusion.30), channel_id=1, replica_groups=mesh['leaf'=32,'front'=16] {'front'}, dimensions={0}, use_global_device_ids=true | all-gather | bytes 557056 | tf_op jit(solution)/shard_map/all_gather | solution.py:60
  587.6 30.3 %all_gather.23 = f32[1024,128]{1,0:T(8,128)S(1)} all-gather(f32[64,128]{1,0:T(8,128)S(1)} %collective-permute-done.2), channel_id=1, replica_groups=mesh['leaf'=32,'front'=16] {'front'}, dimensions={0}, use_global_device_ids=true | all-gather | bytes 557056 | tf_op jit(solution)/shard_map/all_gather | solution.py:61
  617.9 1.0 convolution_add_fusion
  620.7 120.9 %all-reduce.13.cloned.1.call-done = f32[1,2,64,128]{3,2,1,0:T(8,128)} async-done(((f32[1,2,64,128]{3,2,1,0:T(8,128)}), f32[1,2,64,128]{3,2,1,0:T(8,128)}) %all-reduce.13.cloned.1.call-update) | async-done | bytes 65552 | tf_op jit(solution)/shard_map/psum | solution.py:21
  742.6 56.8 %psum.60 = f32[32,128]{1,0:T(8,128)S(1)} all-reduce(f32[32,128]{1,0:T(8,128)S(1)} %convolution_bitcast_fusion.5), channel_id=1, replica_groups=mesh['leaf'=32,'front'=16] {'front'}, use_global_device_ids=true, to_apply=%region_4.5 | all-reduce | flops 4096 | bytes 32768 | tf_op jit(solution)/shard_map/psum | solution.py:126
  799.4 1.9 collective-permute-start.3
  801.3 1.1 collective-permute-done.3
  802.4 3.4 collective-permute-start.4
  805.8 2.4 collective-permute-done.4
  808.2 4.6 collective-permute-start.5
  812.8 3.1 collective-permute-done.5
  815.9 3.3 collective-permute-start.6
  819.3 3.5 collective-permute-done.6
  822.8 4.1 collective-permute-start.7
  827.6 4.9 collective-permute-done.7
  832.7 1.1 fusion.5
  834.2 53.5 %psum.61 = f32[64,128]{1,0:T(8,128)S(1)} all-reduce(f32[64,128]{1,0:T(8,128)S(1)} %convolution_bitcast_fusion.4), channel_id=1, replica_groups=mesh['leaf'=32,'front'=16] {'front'}, use_global_device_ids=true, to_apply=%region_5.6 | all-reduce | flops 8192 | bytes 65536 | tf_op jit(solution)/shard_map/psum | solution.py:126
  887.7 1.9 collective-permute-start.8
  889.6 1.2 collective-permute-done.8
  890.8 3.4 collective-permute-start.9
  894.1 2.8 collective-permute-done.9
  896.9 4.6 collective-permute-start.10
  901.5 3.8 collective-permute-done.10
  905.3 3.5 collective-permute-start.11
  909.8 3.8 collective-permute-done.11
  913.7 1.1 fusion.3
  915.9 129.0 %all-reduce.15.cloned.1.call-done = f32[128,128]{0,1:T(8,128)} async-done(((f32[128,128]{0,1:T(8,128)}), f32[128,128]{0,1:T(8,128)}) %all-reduce.15.cloned.1.call-update) | async-done | bytes 65552 | tf_op jit(solution)/shard_map/psum | solution.py:126
  1044.9 1.9 collective-permute-start.12
  1046.8 1.4 collective-permute-done.12
  1049.1 3.4 collective-permute-start.13
  1053.4 3.2 collective-permute-done.13
  1056.6 4.9 collective-permute-start.14
  1063.1 4.4 collective-permute-done.14
  1068.0 1.1 fusion.1
  1069.2 1.0 convolution_bitcast_fusion
  1071.7 128.7 %all-reduce.17.cloned.1.call-done = f32[256,128]{0,1:T(8,128)} async-done(((f32[256,128]{0,1:T(8,128)}), f32[256,128]{0,1:T(8,128)}) %all-reduce.17.cloned.1.call-update) | async-done | bytes 131088 | tf_op jit(solution)/shard_map/psum | solution.py:126
  (101 shorter events, 25.7 us)
Async XLA Ops:
  7.2 0.9 copy-start
  7.2 142.3 %all-reduce.7.cloned.1.call-start = ((), (), s32[]{:S(2)}) async-start(), calls=%async_computation | async-start | bytes 1048576 | tf_op jit(solution)/shard_map/psum | solution.py:21
  10.2 339.9 %all-reduce.9.cloned.1.call-start = ((), (), s32[]{:S(2)}) async-start(), calls=%async_computation.1 | async-start | bytes 524288 | tf_op jit(solution)/shard_map/psum | solution.py:21
  150.2 38.2 %collective-permute-start = (f32[64,128]{1,0:T(8,128)S(1)}, f32[64,128]{1,0:T(8,128)S(1)}, u32[]{:S(2)}, u32[]{:S(2)}) collective-permute-start(f32[64,128]{1,0:T(8,128)S(1)} %fusion.32), channel_id=1, source_target_pairs={{0,64},{16,80},{32,96},{48,112},{64,0},{80,16},{96,32},{112,48},{1... | collective-permute-start | bytes 98312 | tf_op jit(solution)/shard_map/ppermute | solution.py:12
  220.1 0.8 copy-start.3
  220.1 0.9 copy-start.7
  222.0 325.4 %all-reduce.11.cloned.1.call-start = ((), (), s32[]{:S(2)}) async-start(), calls=%async_computation.2 | async-start | bytes 262144 | tf_op jit(solution)/shard_map/psum | solution.py:21
  350.8 37.5 %collective-permute-start.1 = (f32[64,128]{1,0:T(8,128)S(1)}, f32[64,128]{1,0:T(8,128)S(1)}, u32[]{:S(2)}, u32[]{:S(2)}) collective-permute-start(f32[64,128]{1,0:T(8,128)S(1)} %fusion.31), channel_id=1, source_target_pairs={{0,128},{16,144},{32,160},{48,176},{64,192},{80,208},{96,224},{112... | collective-permute-start | bytes 98312 | tf_op jit(solution)/shard_map/ppermute | solution.py:12
  419.4 0.8 copy-start.2
  419.5 0.8 copy-start.8
  421.2 320.4 %all-reduce.13.cloned.1.call-start = ((), (), s32[]{:S(2)}) async-start(), calls=%async_computation.3 | async-start | bytes 131072 | tf_op jit(solution)/shard_map/psum | solution.py:21
  548.2 39.5 %collective-permute-start.2 = (f32[64,128]{1,0:T(8,128)S(1)}, f32[64,128]{1,0:T(8,128)S(1)}, u32[]{:S(2)}, u32[]{:S(2)}) collective-permute-start(f32[64,128]{1,0:T(8,128)S(1)} %fusion.30), channel_id=1, source_target_pairs={{0,256},{16,272},{32,288},{48,304},{64,320},{80,336},{96,352},{112... | collective-permute-start | bytes 98312 | tf_op jit(solution)/shard_map/ppermute | solution.py:12
  618.9 0.8 copy-start.5
  619.0 0.8 copy-start.9
  619.0 1.7 copy-start.1
  620.7 424.2 %all-reduce.15.cloned.1.call-start = ((), (), s32[]{:S(2)}) async-start(), calls=%async_computation.4 | async-start | bytes 131072 | tf_op jit(solution)/shard_map/psum | solution.py:126
  799.4 3.1 collective-permute-start.3
  802.4 5.8 collective-permute-start.4
  808.2 7.7 collective-permute-start.5
  815.9 6.9 collective-permute-start.6
  822.8 9.8 collective-permute-start.7
  887.7 3.1 collective-permute-start.8
  890.8 6.2 collective-permute-start.9
  896.9 8.4 collective-permute-start.10
  905.3 8.3 collective-permute-start.11
  915.9 284.5 %all-reduce.17.cloned.1.call-start = ((), (), s32[]{:S(2)}) async-start(), calls=%async_computation.5 | async-start | bytes 262144 | tf_op jit(solution)/shard_map/psum | solution.py:126
  1044.9 3.3 collective-permute-start.12
  1049.1 7.5 collective-permute-start.13
  1053.4 8.8 copy-start.6
  1056.6 10.9 collective-permute-start.14
  1070.1 0.8 copy-start.4
Sparse Core Ops, SparseCore 0:
  11.2 138.1 all-reduce.6
  222.1 127.8 all-reduce.8
  421.4 126.0 all-reduce.10
  620.8 120.7 all-reduce.12
  916.0 128.8 all-reduce.14
  1070.3 130.0 all-reduce.16
where the time goes:
time: 1210 us
  waiting for transfers between devices  806 us (67%)
  blocking collectives  301 us (25%)
  starting transfers between devices  53.6 us (4%)
  between operations  14.8 us (1%)
  matrix products  13.7 us (1%)
    psum x4, waiting for transfers between devices, group_total(): totals = lax.psum(spread_out, 'leaf')  513 us
    psum x2, waiting for transfers between devices, on_device(): column_block = lax.psum(partial_sum, 'front')  258 us
    psum x2, blocking collectives, on_device(): column_block = lax.psum(partial_sum, 'front')  110 us
    all_gather x3, blocking collectives, lift_update(): lax.all_gather(update_block, 'front', axis=0, tiled=True)  100 us
    all_gather x3, blocking collectives, lift_update(): lax.all_gather(partner_block, 'front', axis=0, tiled=True)  91 us
    ppermute x15, starting transfers between devices, partner_2(): return lax.ppermute(value, axis, pairs)  53.4 us
    ppermute x15, waiting for transfers between devices, partner_2(): return lax.ppermute(value, axis, pairs)  35.6 us
  transfers between devices with their start and end apart: 21, of which 18 were waited for; matrix products, arithmetic and copies ran while one was open for 1% of the time, Pallas kernels for 0%

commit v1 on v0

--- a/solution.py
+++ b/solution.py
@@ -18,7 +18,7 @@
     slot_id = leaf_pos >> group_bits
     chosen = (jnp.arange(group_count, dtype=jnp.int32) == slot_id).astype(jnp.float32)
     spread_out = chosen.reshape((group_count,) + (1,) * partial_sum.ndim) * partial_sum[None]
-    totals = lax.psum(spread_out, "leaf")
+    totals = jnp.sum(lax.all_gather(spread_out, "leaf"), axis=0)
     return lax.dynamic_index_in_dim(totals, slot_id, 0, keepdims=False)
 
 

time: 1210 us -> 982 us (0.81)
  waiting for transfers between devices: 806 us -> 579 us
  other arithmetic: 6.93 us -> 21.2 us
    psum x4 -> x0, waiting for transfers between devices: 513 us -> none  [group_total(): totals = lax.psum(spread_out, 'leaf')]
    all_gather x0 -> x4, waiting for transfers between devices: none -> 270 us  [group_total(): totals = jnp.sum(lax.all_gather(spread_out, 'leaf'), axis=0)]
    ppermute x15, waiting for transfers between devices: 35.6 us -> 51.8 us  [partner_2(): return lax.ppermute(value, axis, pairs)]
    reduce_sum x0 -> x4, other arithmetic: none -> 15.6 us  [group_total(): totals = jnp.sum(lax.all_gather(spread_out, 'leaf'), axis=0)]
  transfers between devices with their start and end apart: 21 -> 21, of which waited for: 18 -> 21; matrix products, arithmetic and copies ran while one was open for 1% -> 1% of each run, Pallas kernels for 0% -> 0%
where the time goes in v1:
time: 982 us; the launch traced here: 981 us
  waiting for transfers between devices  579 us (59%)
  blocking collectives  300 us (31%)
  starting transfers between devices  45 us (5%)
  other arithmetic  21.2 us (2%)
  between operations  14.8 us (2%)
  matrix products  13.7 us (1%)
    all_gather x4, waiting for transfers between devices, group_total(): totals = jnp.sum(lax.all_gather(spread_out, 'leaf'), axis=0)  270 us
    psum x2, waiting for transfers between devices, on_device(): column_block = lax.psum(partial_sum, 'front')  258 us
    psum x2, blocking collectives, on_device(): column_block = lax.psum(partial_sum, 'front')  110 us
    all_gather x3, blocking collectives, lift_update(): lax.all_gather(update_block, 'front', axis=0, tiled=True)  101 us
    all_gather x3, blocking collectives, lift_update(): lax.all_gather(partner_block, 'front', axis=0, tiled=True)  89.1 us
    ppermute x15, waiting for transfers between devices, partner_2(): return lax.ppermute(value, axis, pairs)  51.8 us
    ppermute x15, starting transfers between devices, partner_2(): return lax.ppermute(value, axis, pairs)  44.8 us
  transfers between devices with their start and end apart: 21, of which 21 were waited for; matrix products, arithmetic and copies ran while one was open for 1% of the time, Pallas kernels for 0%

profile of v1, /device:TPU:2, one launch (start us, length us, event | category | flops | bytes accessed | tf_op | source)
XLA Modules:
  0.0 981.1 jit_solution(546427932062317067)
XLA Ops:
  8.1 1.2 fusion.16
  11.2 92.3 %all-gather.6.cloned.1.call-done = f32[32,8,2,64,128]{4,3,2,1,0:T(8,128)} async-done(((f32[1,8,2,64,128]{4,3,2,1,0:T(8,128)}), f32[32,8,2,64,128]{4,3,2,1,0:T(8,128)}) %all-gather.6.cloned.1.call-update) | async-done | bytes 16777232 | tf_op jit(solution)/shard_map/all_gather | solution.py:21
  103.4 7.5 reduce_sum.38
  111.7 33.5 %all_gather.37 = f32[1024,128]{1,0:T(8,128)S(1)} all-gather(f32[64,128]{1,0:T(8,128)S(1)} %fusion.30), channel_id=1, replica_groups=mesh['leaf'=32,'front'=16] {'front'}, dimensions={0}, use_global_device_ids=true | all-gather | bytes 557056 | tf_op jit(solution)/shard_map/all_gather | solution.py:60
  145.2 3.2 collective-permute-start
  149.3 3.2 collective-permute-done
  152.5 29.7 %all_gather.38 = f32[1024,128]{1,0:T(8,128)S(1)} all-gather(f32[64,128]{1,0:T(8,128)S(1)} %collective-permute-done), channel_id=1, replica_groups=mesh['leaf'=32,'front'=16] {'front'}, dimensions={0}, use_global_device_ids=true | all-gather | bytes 557056 | tf_op jit(solution)/shard_map/all_gather | solution.py:61
  184.6 64.6 %all-gather.8.cloned.1.call-done = f32[32,4,2,64,128]{4,3,2,1,0:T(8,128)} async-done(((f32[1,4,2,64,128]{4,3,2,1,0:T(8,128)}), f32[32,4,2,64,128]{4,3,2,1,0:T(8,128)}) %all-gather.8.cloned.1.call-update) | async-done | bytes 8388624 | tf_op jit(solution)/shard_map/all_gather | solution.py:21
  249.2 4.0 reduce_sum.39
  253.2 33.5 %all_gather.40 = f32[1024,128]{1,0:T(8,128)S(1)} all-gather(f32[64,128]{1,0:T(8,128)S(1)} %fusion.29), channel_id=1, replica_groups=mesh['leaf'=32,'front'=16] {'front'}, dimensions={0}, use_global_device_ids=true | all-gather | bytes 557056 | tf_op jit(solution)/shard_map/all_gather | solution.py:60
  286.8 2.5 collective-permute-start.1
  290.1 2.4 collective-permute-done.1
  292.6 29.7 %all_gather.41 = f32[1024,128]{1,0:T(8,128)S(1)} all-gather(f32[64,128]{1,0:T(8,128)S(1)} %collective-permute-done.1), channel_id=1, replica_groups=mesh['leaf'=32,'front'=16] {'front'}, dimensions={0}, use_global_device_ids=true | all-gather | bytes 557056 | tf_op jit(solution)/shard_map/all_gather | solution.py:61
  324.6 57.5 %all-gather.10.cloned.1.call-done = f32[32,2,2,64,128]{4,3,2,1,0:T(8,128)} async-done(((f32[1,2,2,64,128]{4,3,2,1,0:T(8,128)}), f32[32,2,2,64,128]{4,3,2,1,0:T(8,128)}) %all-gather.10.cloned.1.call-update) | async-done | bytes 4194320 | tf_op jit(solution)/shard_map/all_gather | solution.py:21
  382.1 2.4 reduce_sum.40
  384.5 33.5 %all_gather.43 = f32[1024,128]{1,0:T(8,128)S(1)} all-gather(f32[64,128]{1,0:T(8,128)S(1)} %fusion.28), channel_id=1, replica_groups=mesh['leaf'=32,'front'=16] {'front'}, dimensions={0}, use_global_device_ids=true | all-gather | bytes 557056 | tf_op jit(solution)/shard_map/all_gather | solution.py:60
  418.1 3.9 collective-permute-start.2
  422.9 2.5 collective-permute-done.2
  425.4 29.7 %all_gather.44 = f32[1024,128]{1,0:T(8,128)S(1)} all-gather(f32[64,128]{1,0:T(8,128)S(1)} %collective-permute-done.2), channel_id=1, replica_groups=mesh['leaf'=32,'front'=16] {'front'}, dimensions={0}, use_global_device_ids=true | all-gather | bytes 557056 | tf_op jit(solution)/shard_map/all_gather | solution.py:61
  457.3 55.4 %all-gather.12.cloned.1.call-done = f32[64,64,128]{2,1,0:T(8,128)} async-done(((f32[2,64,128]{2,1,0:T(8,128)}), f32[64,64,128]{2,1,0:T(8,128)}) %all-gather.12.cloned.1.call-update) | async-done | bytes 2097168 | tf_op jit(solution)/shard_map/all_gather | solution.py:21
  512.7 1.7 reduce.1
  514.6 56.8 %psum.28 = f32[32,128]{1,0:T(8,128)S(1)} all-reduce(f32[32,128]{1,0:T(8,128)S(1)} %convolution_bitcast_fusion.5), channel_id=1, replica_groups=mesh['leaf'=32,'front'=16] {'front'}, use_global_device_ids=true, to_apply=%region_4.5 | all-reduce | flops 4096 | bytes 32768 | tf_op jit(solution)/shard_map/psum | solution.py:126
  571.4 1.9 collective-permute-start.3
  574.5 2.2 collective-permute-start.4
  576.7 3.6 collective-permute-done.4
  580.3 3.4 collective-permute-start.5
  583.7 4.3 collective-permute-done.5
  588.0 2.9 collective-permute-start.6
  590.9 4.0 collective-permute-done.6
  594.9 4.2 collective-permute-start.7
  599.1 5.6 collective-permute-done.7
  606.2 53.5 %psum.29 = f32[64,128]{1,0:T(8,128)S(1)} all-reduce(f32[64,128]{1,0:T(8,128)S(1)} %convolution_bitcast_fusion.4), channel_id=1, replica_groups=mesh['leaf'=32,'front'=16] {'front'}, use_global_device_ids=true, to_apply=%region_5.6 | all-reduce | flops 8192 | bytes 65536 | tf_op jit(solution)/shard_map/psum | solution.py:126
  659.7 1.9 collective-permute-start.8
  661.6 1.2 collective-permute-done.8
  662.8 2.2 collective-permute-start.9
  665.0 4.0 collective-permute-done.9
  669.0 3.4 collective-permute-start.10
  672.4 5.0 collective-permute-done.10
  677.4 2.9 collective-permute-start.11
  680.5 5.2 collective-permute-done.11
  688.0 129.0 %all-reduce.3.cloned.1.call-done = f32[128,128]{0,1:T(8,128)} async-done(((f32[128,128]{0,1:T(8,128)}), f32[128,128]{0,1:T(8,128)}) %all-reduce.3.cloned.1.call-update) | async-done | bytes 65552 | tf_op jit(solution)/shard_map/psum | solution.py:126
  816.9 2.0 collective-permute-start.12
  819.0 1.4 collective-permute-done.12
  821.4 3.4 collective-permute-start.13
  824.8 4.0 collective-permute-done.13
  828.8 4.9 collective-permute-start.14
  835.3 4.4 collective-permute-done.14
  843.8 128.9 %all-reduce.5.cloned.1.call-done = f32[256,128]{0,1:T(8,128)} async-done(((f32[256,128]{0,1:T(8,128)}), f32[256,128]{0,1:T(8,128)}) %all-reduce.5.cloned.1.call-update) | async-done | bytes 131088 | tf_op jit(solution)/shard_map/psum | solution.py:126
  (103 shorter events, 26.5 us)
Async XLA Ops:
  7.2 0.9 copy-start
  7.2 96.2 %all-gather.6.cloned.1.call-start = ((), (), s32[]{:S(2)}) async-start(), calls=%async_computation | async-start | bytes 17301504 | tf_op jit(solution)/shard_map/all_gather | solution.py:21
  10.2 239.0 %all-gather.8.cloned.1.call-start = ((), (), s32[]{:S(2)}) async-start(), calls=%async_computation.1 | async-start | bytes 8650752 | tf_op jit(solution)/shard_map/all_gather | solution.py:21
  11.2 172.3 %copy-start.3 = (f32[2,64,128]{2,1,0:T(8,128)S(1)}, f32[2,64,128]{2,1,0:T(8,128)}, u32[]{:S(2)}) copy-start(f32[2,64,128]{2,1,0:T(8,128)} %param.13) | copy-start | bytes 196612
  11.2 172.3 %copy-start.6 = (f32[128,128]{1,0:T(8,128)S(1)}, f32[128,128]{1,0:T(8,128)}, u32[]{:S(2)}) copy-start(f32[128,128]{1,0:T(8,128)} %param.17) | copy-start | bytes 196612
  145.2 7.3 collective-permute-start
  183.6 139.8 %copy-start.2 = (f32[2,64,64]{2,1,0:T(8,128)S(1)}, f32[2,64,64]{2,1,0:T(8,128)}, u32[]{:S(2)}) copy-start(f32[2,64,64]{2,1,0:T(8,128)} %param.12) | copy-start | bytes 98308
  183.7 139.8 %copy-start.7 = (f32[64,128]{1,0:T(8,128)S(1)}, f32[64,128]{1,0:T(8,128)}, u32[]{:S(2)}) copy-start(f32[64,128]{1,0:T(8,128)} %param.16) | copy-start | bytes 98308
  184.5 197.6 %all-gather.10.cloned.1.call-start = ((), (), s32[]{:S(2)}) async-start(), calls=%async_computation.2 | async-start | bytes 4325376 | tf_op jit(solution)/shard_map/all_gather | solution.py:21
  286.8 5.8 collective-permute-start.1
  322.3 134.0 %copy-start.5 = (f32[2,64,32]{1,2,0:T(8,128)S(1)}, f32[2,64,32]{1,2,0:T(8,128)}, u32[]{:S(2)}) copy-start(f32[2,64,32]{1,2,0:T(8,128)} %param.11) | copy-start | bytes 49156
  322.3 134.0 %copy-start.8 = (f32[32,128]{1,0:T(8,128)S(1)}, f32[32,128]{1,0:T(8,128)}, u32[]{:S(2)}) copy-start(f32[32,128]{1,0:T(8,128)} %param.15) | copy-start | bytes 49156
  322.3 135.0 %copy-start.1 = (f32[1024,128]{1,0:T(8,128)S(1)}, f32[1024,128]{1,0:T(8,128)}, u32[]{:S(2)}) copy-start(f32[1024,128]{1,0:T(8,128)} %param.20) | copy-start | bytes 1572868
  324.5 188.2 %all-gather.12.cloned.1.call-start = ((), (), s32[]{:S(2)}) async-start(), calls=%async_computation.5 | async-start | bytes 2162688 | tf_op jit(solution)/shard_map/all_gather | solution.py:21
  418.1 7.3 collective-permute-start.2
  457.3 359.7 %all-reduce.3.cloned.1.call-start = ((), (), s32[]{:S(2)}) async-start(), calls=%async_computation.3 | async-start | bytes 131072 | tf_op jit(solution)/shard_map/psum | solution.py:126
  571.4 3.1 collective-permute-start.3
  574.5 5.8 collective-permute-start.4
  580.3 7.7 collective-permute-start.5
  588.0 6.9 collective-permute-start.6
  594.9 9.8 collective-permute-start.7
  659.7 3.1 collective-permute-start.8
  662.8 6.2 collective-permute-start.9
  669.0 8.4 collective-permute-start.10
  677.4 8.3 collective-permute-start.11
  687.9 284.8 %all-reduce.5.cloned.1.call-start = ((), (), s32[]{:S(2)}) async-start(), calls=%async_computation.4 | async-start | bytes 262144 | tf_op jit(solution)/shard_map/psum | solution.py:126
  816.9 26.1 %copy-start.4 = (f32[128,128]{0,1:T(8,128)S(1)}, f32[128,128]{0,1:T(8,128)}, u32[]{:S(2)}) copy-start(f32[128,128]{0,1:T(8,128)} %all-reduce.3.cloned.1.call-done) | copy-start | bytes 196612
  816.9 3.5 collective-permute-start.12
  821.4 7.5 collective-permute-start.13
  828.8 10.9 %collective-permute-start.14 = (f32[512,128]{0,1:T(8,128)S(1)}, f32[512,128]{0,1:T(8,128)S(1)}, u32[]{:S(2)}, u32[]{:S(2)}) collective-permute-start(f32[512,128]{0,1:T(8,128)S(1)} %maximum_select_fusion.5), channel_id=1, source_target_pairs={{0,64},{16,80},{32,96},{48,112},{64,0},{80,16},{96,32},{112,48},{1... | collective-permute-start | bytes 786440 | tf_op jit(solution)/shard_map/ppermute | solution.py:12
Sparse Core Ops, SparseCore 0:
  11.2 92.2 all-gather.5
  184.6 64.5 all-gather.7
  324.6 57.4 all-gather.9
  457.4 55.2 all-gather.11
  688.0 128.8 all-reduce.2
  842.6 130.0 all-reduce.4
